TPU v7x, 32 devices: a whole 2x2x4 slice. The times are simulated.
32 devices in a mesh: dp: 4 (over y, x), sp: 8 (over z, core).
Axes of the slice: x: 2, y: 2, z: 4, core: 2. Of those that a mesh axis runs over, the one named last changes fastest.
Arguments:
- tokens: bfloat16 [4, 2048, 1152], P('dp', 'sp'), may hold values from -6 to 6
- image_len: int32 [4, 8], P('dp'), may hold values from 0 to 1024, as said below
- timestep: int32 [4, 8], P('dp'), may hold values from 0 to 63
- caption: bfloat16 [4, 120, 1152], P('dp'), may hold values from -6 to 6
- time_embed: float32 [64, 6912], replicated, may hold values from -6 to 6
- mod_table: float32 [6, 1152], replicated, may hold values from -6 to 6
- w_qkv: bfloat16 [1152, 3456], replicated, may hold values from -0.1875 to 0.1875
- w_out: bfloat16 [1152, 1152], replicated, may hold values from -0.5 to 0.5
- cross_q: bfloat16 [1152, 1152], replicated, may hold values from -0.1875 to 0.1875
- cross_kv: bfloat16 [1152, 2304], replicated, may hold values from -0.1875 to 0.1875
- cross_out: bfloat16 [1152, 1152], replicated, may hold values from -0.375 to 0.375
- w_up: bfloat16 [1152, 4608], replicated, may hold values from -0.1875 to 0.1875
- w_down: bfloat16 [4608, 1152], replicated, may hold values from -0.09375 to 0.09375
- cotangent: bfloat16 [4, 2048, 1152], P('dp', 'sp'), may hold values from -6 to 6
Outputs:
- out_tokens: float32 [4, 2048, 1152], P('dp', 'sp')
- grad_tokens: float32 [4, 2048, 1152], P('dp', 'sp')
- grad_table: float32 [6912], P(('dp', 'sp'))
- grad_qkv: float32 [1152, 3456], P('dp', 'sp')
- grad_out: float32 [1152, 1152], P('dp', 'sp')
- grad_cross_q: float32 [1152, 1152], P('dp', 'sp')
- grad_cross_kv: float32 [1152, 2304], P('dp', 'sp')
- grad_cross_out: float32 [1152, 1152], P('dp', 'sp')
- grad_up: float32 [1152, 4608], P('dp', 'sp')
- grad_down: float32 [4608, 1152], P('dp', 'sp')
Inputs may be any that keep to these rules, and one draw needn't show every extreme that they name: `image_len`: each row lists its images' patch counts, each 256 or 1024, followed by zeros; a row's counts sum to 2048, and every row holds at least one image of 1024 patches.
All inputs are finite; a program needn't handle non-finite values.
Results may differ from a plain program's by a relative error of at most 0.02.
Values may be sent and summed in bfloat16 or wider, within the bound.
No kernel may reach another device: no remote copies, remote signals or barrier semaphores. Data moves between devices by JAX's collectives and lax.ppermute only.
A program may use at most 320 MiB of HBM per device.

v0:
```python
import math

import jax
import jax.numpy as jnp
from jax import lax
from jax.sharding import PartitionSpec as P

HEADS = 16


EPS = 1e-06
BIGNEG = -1e30
HIGH = lax.Precision.HIGHEST


def normed(stream, shift, scale):
    centred = stream - jnp.mean(stream, axis=-1, keepdims=True)
    spread = jnp.mean(centred * centred, axis=-1, keepdims=True)
    return centred * lax.rsqrt(spread + EPS) * (1.0 + scale) + shift


def matmul(left, right):
    return jnp.dot(left, right, preferred_element_type=jnp.float32)


def matmul_tn(left, right):
    return lax.dot_general(
        left, right, (((0,), (0,)), ((), ())), preferred_element_type=jnp.float32
    )


def matmul_nt(left, right):
    return lax.dot_general(
        left, right, (((1,), (1,)), ((), ())), preferred_element_type=jnp.float32
    )


def self_attend(head_rows, labels, factor):
    queries = head_rows[:, 0]
    key_rows = head_rows[:, 1]
    value_rows = head_rows[:, 2]
    total_rows = queries.shape[0]
    block_rows = min(512, total_rows)
    block_count = total_rows // block_rows

    def one_block(items_in):
        query_block, query_label = items_in
        scores = (
            jnp.einsum("qhd,khd->hqk", query_block, key_rows, preferred_element_type=jnp.float32)
            * factor
        )
        allowed = (query_label[:, None] == labels[None, :])[None]
        scores = jnp.where(allowed, scores, BIGNEG)
        row_max = jnp.max(scores, axis=-1, keepdims=True)
        raised = jnp.exp(scores - row_max)
        row_total = jnp.sum(raised, axis=-1, keepdims=True)
        weights = (raised / row_total).astype(jnp.bfloat16)
        result = jnp.einsum("hqk,khd->qhd", weights, value_rows, preferred_element_type=jnp.float32)
        return (result.astype(jnp.bfloat16), (row_max + jnp.log(row_total))[..., 0])

    outputs, logsum = lax.map(
        one_block,
        (
            queries.reshape(block_count, block_rows, queries.shape[1], queries.shape[2]),
            labels.reshape(block_count, block_rows),
        ),
    )
    return (outputs.reshape(queries.shape), logsum)


def self_attend_back(head_rows, logsum, grad_rows, labels, factor):
    queries = head_rows[:, 0]
    key_rows = head_rows[:, 1]
    value_rows = head_rows[:, 2]
    total_rows = queries.shape[0]
    block_rows = min(512, total_rows)
    block_count = total_rows // block_rows

    def one_block(running, items_in):
        grad_keys, grad_values = running
        query_block, grad_block, block_sum, query_label = items_in
        scores = (
            jnp.einsum("qhd,khd->hqk", query_block, key_rows, preferred_element_type=jnp.float32)
            * factor
        )
        allowed = (query_label[:, None] == labels[None, :])[None]
        scores = jnp.where(allowed, scores, BIGNEG)
        prob_rows = jnp.exp(scores - block_sum[..., None])
        weights = prob_rows.astype(jnp.bfloat16)
        grad_weights = jnp.einsum(
            "qhd,khd->hqk", grad_block, value_rows, preferred_element_type=jnp.float32
        )
        inner_sum = jnp.sum(prob_rows * grad_weights, axis=-1, keepdims=True)
        grad_scores = (prob_rows * (grad_weights - inner_sum)).astype(jnp.bfloat16)
        grad_query = (
            jnp.einsum("hqk,khd->qhd", grad_scores, key_rows, preferred_element_type=jnp.float32)
            * factor
        )
        grad_keys = (
            grad_keys
            + jnp.einsum(
                "hqk,qhd->khd", grad_scores, query_block, preferred_element_type=jnp.float32
            )
            * factor
        )
        grad_values = grad_values + jnp.einsum(
            "hqk,qhd->khd", weights, grad_block, preferred_element_type=jnp.float32
        )
        return ((grad_keys, grad_values), grad_query)

    zero_rows = jnp.zeros(key_rows.shape, jnp.float32)
    shape_blocks = (block_count, block_rows, queries.shape[1], queries.shape[2])
    (grad_keys, grad_values), grad_queries = lax.scan(
        one_block,
        (zero_rows, zero_rows),
        (
            queries.reshape(shape_blocks),
            grad_rows.reshape(shape_blocks),
            logsum,
            labels.reshape(block_count, block_rows),
        ),
    )
    return (grad_queries.reshape(queries.shape), grad_keys, grad_values)


def local(
    tokens,
    image_len,
    timestep,
    caption,
    time_embed,
    mod_table,
    w_qkv,
    w_out,
    cross_q,
    cross_kv,
    cross_out,
    w_up,
    w_down,
    cotangent,
):
    sp_count = lax.axis_size("sp")
    dp_count = lax.axis_size("dp")
    sp_place = lax.axis_index("sp")
    stream_in = tokens[0].astype(jnp.float32)
    local_rows = stream_in.shape[0]
    model_width = stream_in.shape[1]
    row_len = local_rows * sp_count
    head_size = model_width // HEADS
    factor = 1.0 / math.sqrt(head_size)
    image_ends = jnp.cumsum(image_len[0])
    places = jnp.arange(row_len, dtype=jnp.int32)
    labels = jnp.sum((image_ends[None, :] <= places[:, None]).astype(jnp.int32), axis=1)
    own_labels = lax.dynamic_slice_in_dim(labels, sp_place * local_rows, local_rows)
    step_pick = (
        timestep[0][:, None] == jnp.arange(time_embed.shape[0], dtype=jnp.int32)[None, :]
    ).astype(jnp.float32)
    slot_mod = jnp.dot(step_pick, time_embed, precision=HIGH)
    slot_pick = (
        own_labels[:, None] == jnp.arange(image_len.shape[1], dtype=jnp.int32)[None, :]
    ).astype(jnp.float32)
    modulation = (
        jnp.dot(slot_pick, slot_mod, precision=HIGH).reshape(local_rows, 6, model_width)
        + mod_table[None]
    )
    shift_one = modulation[:, 0]
    scale_one = modulation[:, 1]
    gate_one = modulation[:, 2]
    shift_two = modulation[:, 3]
    scale_two = modulation[:, 4]
    gate_two = modulation[:, 5]
    caption_rows = caption[0]
    text_kv = matmul(caption_rows, cross_kv)
    text_keys = text_kv[:, :model_width].astype(jnp.bfloat16).reshape(-1, HEADS, head_size)
    text_values = text_kv[:, model_width:].astype(jnp.bfloat16).reshape(-1, HEADS, head_size)

    def forward(stream):
        first_in = normed(stream, shift_one, scale_one).astype(jnp.bfloat16)
        projected = (
            matmul(first_in, w_qkv).astype(jnp.bfloat16).reshape(local_rows, 3, HEADS, head_size)
        )
        head_rows = lax.all_to_all(projected, "sp", split_axis=2, concat_axis=0, tiled=True)
        attended, logsum = self_attend(head_rows, labels, factor)
        back_rows = lax.all_to_all(attended, "sp", split_axis=0, concat_axis=1, tiled=True).reshape(
            local_rows, model_width
        )
        attn_branch = matmul(back_rows, w_out)
        stream_one = stream + gate_one * attn_branch
        cross_in = stream_one.astype(jnp.bfloat16)
        cross_queries = (
            matmul(cross_in, cross_q).astype(jnp.bfloat16).reshape(local_rows, HEADS, head_size)
        )
        cross_scores = (
            jnp.einsum("qhd,khd->hqk", cross_queries, text_keys, preferred_element_type=jnp.float32)
            * factor
        )
        row_max = jnp.max(cross_scores, axis=-1, keepdims=True)
        raised = jnp.exp(cross_scores - row_max)
        cross_probs = raised / jnp.sum(raised, axis=-1, keepdims=True)
        cross_weights = cross_probs.astype(jnp.bfloat16)
        cross_mixed = (
            jnp.einsum(
                "hqk,khd->qhd", cross_weights, text_values, preferred_element_type=jnp.float32
            )
            .astype(jnp.bfloat16)
            .reshape(local_rows, model_width)
        )
        cross_branch = matmul(cross_mixed, cross_out)
        stream_two = stream_one + cross_branch
        second_in = normed(stream_two, shift_two, scale_two).astype(jnp.bfloat16)
        hidden_pre = matmul(second_in, w_up)
        hidden = jax.nn.gelu(hidden_pre, approximate=True).astype(jnp.bfloat16)
        mlp_branch = matmul(hidden, w_down)
        stream_three = stream_two + gate_two * mlp_branch
        kept_state = (
            first_in,
            head_rows,
            logsum,
            back_rows,
            attn_branch,
            cross_in,
            cross_queries,
            cross_probs,
            cross_weights,
            cross_mixed,
            stream_two,
            second_in,
            hidden_pre,
            hidden,
            mlp_branch,
        )
        return (stream_three, kept_state)

    stream_three, kept_state = forward(stream_in)
    again_input = lax.optimization_barrier((stream_in, stream_three))[0]
    saved_state = forward(again_input)[1]
    (
        first_in,
        head_rows,
        logsum,
        back_rows,
        attn_branch,
        cross_in,
        cross_queries,
        cross_probs,
        cross_weights,
        cross_mixed,
        stream_two,
        second_in,
        hidden_pre,
        hidden,
        mlp_branch,
    ) = saved_state
    grad_three = cotangent[0].astype(jnp.float32)
    grad_gate_two = grad_three * mlp_branch
    grad_mlp = (gate_two * grad_three).astype(jnp.bfloat16)
    grad_down = matmul_tn(hidden, grad_mlp)
    grad_hidden = matmul_nt(grad_mlp, w_down)
    gelu_pull = jax.vjp(lambda preact: jax.nn.gelu(preact, approximate=True), hidden_pre)[1]
    grad_pre = gelu_pull(grad_hidden)[0].astype(jnp.bfloat16)
    grad_up = matmul_tn(second_in, grad_pre)
    grad_second = matmul_nt(grad_pre, w_up)
    second_pull = jax.vjp(normed, stream_two, shift_two, scale_two)[1]
    grad_norm_two, grad_shift_two, grad_scale_two = second_pull(grad_second)
    grad_stream_two = grad_three + grad_norm_two
    grad_cross = grad_stream_two.astype(jnp.bfloat16)
    grad_cross_out = matmul_tn(cross_mixed, grad_cross)
    grad_mixed = (
        matmul_nt(grad_cross, cross_out).astype(jnp.bfloat16).reshape(local_rows, HEADS, head_size)
    )
    grad_cross_w = jnp.einsum(
        "qhd,khd->hqk", grad_mixed, text_values, preferred_element_type=jnp.float32
    )
    grad_text_values = jnp.einsum(
        "hqk,qhd->khd", cross_weights, grad_mixed, preferred_element_type=jnp.float32
    )
    inner_sum = jnp.sum(cross_probs * grad_cross_w, axis=-1, keepdims=True)
    grad_cross_scores = (cross_probs * (grad_cross_w - inner_sum)).astype(jnp.bfloat16)
    grad_cross_queries = (
        (
            jnp.einsum(
                "hqk,khd->qhd", grad_cross_scores, text_keys, preferred_element_type=jnp.float32
            )
            * factor
        )
        .astype(jnp.bfloat16)
        .reshape(local_rows, model_width)
    )
    grad_text_keys = (
        jnp.einsum(
            "hqk,qhd->khd", grad_cross_scores, cross_queries, preferred_element_type=jnp.float32
        )
        * factor
    )
    grad_text = jnp.concatenate(
        [grad_text_keys.reshape(-1, model_width), grad_text_values.reshape(-1, model_width)], axis=1
    )
    grad_cross_kv = jnp.dot(caption_rows.astype(jnp.float32).T, grad_text, precision=HIGH)
    grad_cross_q = matmul_tn(cross_in, grad_cross_queries)
    grad_stream_one = grad_stream_two + matmul_nt(grad_cross_queries, cross_q)
    grad_gate_one = grad_stream_one * attn_branch
    grad_attn = (gate_one * grad_stream_one).astype(jnp.bfloat16)
    grad_w_out = matmul_tn(back_rows, grad_attn)
    grad_back = (
        matmul_nt(grad_attn, w_out).astype(jnp.bfloat16).reshape(local_rows, HEADS, head_size)
    )
    grad_heads_out = lax.all_to_all(grad_back, "sp", split_axis=1, concat_axis=0, tiled=True)
    grad_queries, grad_keys, grad_values = self_attend_back(
        head_rows, logsum, grad_heads_out, labels, factor
    )
    grad_proj = jnp.stack([grad_queries, grad_keys, grad_values], axis=1).astype(jnp.bfloat16)
    grad_local = lax.all_to_all(grad_proj, "sp", split_axis=0, concat_axis=2, tiled=True).reshape(
        local_rows, 3 * model_width
    )
    grad_qkv = matmul_tn(first_in, grad_local)
    grad_first = matmul_nt(grad_local, w_qkv)
    first_pull = jax.vjp(normed, stream_in, shift_one, scale_one)[1]
    grad_norm_one, grad_shift_one, grad_scale_one = first_pull(grad_first)
    grad_tokens = grad_stream_one + grad_norm_one
    grad_modulation = jnp.stack(
        [
            grad_shift_one,
            grad_scale_one,
            grad_gate_one,
            grad_shift_two,
            grad_scale_two,
            grad_gate_two,
        ],
        axis=1,
    )
    table_sum = jnp.sum(grad_modulation, axis=0).reshape(-1)
    arranged = table_sum.reshape(dp_count, sp_count, -1).transpose(1, 0, 2).reshape(-1)
    part_qkv, part_out, part_cq, part_ckv, part_co, part_up, part_down, part_table = (
        lax.psum_scatter(grad_qkv, "sp", scatter_dimension=1, tiled=True),
        lax.psum_scatter(grad_w_out, "sp", scatter_dimension=1, tiled=True),
        lax.psum_scatter(grad_cross_q, "sp", scatter_dimension=1, tiled=True),
        lax.psum_scatter(grad_cross_kv, "sp", scatter_dimension=1, tiled=True),
        lax.psum_scatter(grad_cross_out, "sp", scatter_dimension=1, tiled=True),
        lax.psum_scatter(grad_up, "sp", scatter_dimension=1, tiled=True),
        lax.psum_scatter(grad_down, "sp", scatter_dimension=1, tiled=True),
        lax.psum_scatter(arranged, "sp", scatter_dimension=0, tiled=True),
    )
    final_qkv, final_out, final_cq, final_ckv, final_co, final_up, final_down, final_table = (
        lax.psum_scatter(part_qkv, "dp", scatter_dimension=0, tiled=True),
        lax.psum_scatter(part_out, "dp", scatter_dimension=0, tiled=True),
        lax.psum_scatter(part_cq, "dp", scatter_dimension=0, tiled=True),
        lax.psum_scatter(part_ckv, "dp", scatter_dimension=0, tiled=True),
        lax.psum_scatter(part_co, "dp", scatter_dimension=0, tiled=True),
        lax.psum_scatter(part_up, "dp", scatter_dimension=0, tiled=True),
        lax.psum_scatter(part_down, "dp", scatter_dimension=0, tiled=True),
        lax.psum_scatter(part_table, "dp", scatter_dimension=0, tiled=True),
    )
    return (
        stream_three[None],
        grad_tokens[None],
        final_table,
        final_qkv,
        final_out,
        final_cq,
        final_ckv,
        final_co,
        final_up,
        final_down,
    )


def solution(mesh):
    return jax.shard_map(
        local,
        mesh=mesh,
        in_specs=(
            P("dp", "sp", None),
            P("dp", None),
            P("dp", None),
            P("dp", None, None),
            P(),
            P(),
            P(),
            P(),
            P(),
            P(),
            P(),
            P(),
            P(),
            P("dp", "sp", None),
        ),
        out_specs=(
            P("dp", "sp", None),
            P("dp", "sp", None),
            P(("dp", "sp")),
            P("dp", "sp"),
            P("dp", "sp"),
            P("dp", "sp"),
            P("dp", "sp"),
            P("dp", "sp"),
            P("dp", "sp"),
            P("dp", "sp"),
        ),
        check_vma=False,
    )
```

profile of v0, /device:TPU:0, one launch (start us, length us, event | category | flops | bytes accessed | tf_op | source)
XLA Modules:
  0.0 1668.5 jit_solution(2166525651948481538)
XLA Ops:
  15.7 8.1 copy.159
  48.3 42.1 %all-to-all-done = bf16[256,3,16,72]{0,3,1,2:T(8,128)(2,1)} async-done(((bf16[256,3,16,72]{0,3,1,2:T(8,128)(2,1)}), bf16[256,3,16,72]{0,3,1,2:T(8,128)(2,1)}, u32[]{:S(2)}, u32[]{:S(2)}) %all-to-all-start) | async-done | bytes 1769504 | tf_op jit(solution)/shard_map/all_to_all | solution.py:182
  105.7 60.7 %while.37 = (s32[]{:T(128)}, bf16[4,512,2,72]{1,3,2,0:T(8,128)(2,1)}, s32[4,512]{1,0:T(4,128)S(1)}, s32[2048]{0:T(1024)S(1)}, bf16[4,512,2,72]{1,3,2,0:T(8,128)(...) while((s32[]{:T(128)}, bf16[4,512,2,72]{1,3,2,0:T(8,128)(2,1)}, ...), condition=%wide.region_7.8_spmd, body=%wide.region_4.7_spmd.sunk | while | flops 617687040 | bytes 20372568 | solution.py:61
  107.4 8.0 fusion.261
  122.6 8.0 fusion.261
  137.7 8.0 fusion.261
  152.9 8.0 fusion.261
  182.7 18.2 %all-to-all-done.1 = bf16[2048,2,72]{2,1,0:T(2,128)(2,1)} async-done(((bf16[2048,2,72]{2,1,0:T(2,128)(2,1)}), bf16[2048,2,72]{2,1,0:T(2,128)(2,1)}, u32[]{:S(2)}, u32[]{:S(2)}) %all-to-all-start.1) | async-done | bytes 589856 | tf_op jit(solution)/shard_map/all_to_all | solution.py:184
  220.1 16.1 fusion.88
  260.5 42.0 %all-to-all-done.2 = bf16[256,3,16,72]{0,3,1,2:T(8,128)(2,1)} async-done(((bf16[256,3,16,72]{0,3,1,2:T(8,128)(2,1)}), bf16[256,3,16,72]{0,3,1,2:T(8,128)(2,1)}, u32[]{:S(2)}, u32[]{:S(2)}) %all-to-all-start.2) | async-done | bytes 1769504 | tf_op jit(solution)/shard_map/all_to_all | solution.py:182
  317.8 40.9 %while.38 = (s32[]{:T(128)}, bf16[4,512,2,72]{1,3,2,0:T(8,128)(2,1)}, f32[4,2,512]{2,1,0:T(2,128)}, s32[4,512]{1,0:T(4,128)S(1)}, s32[2048]{0:T(1024)S(1)}, /*in...) while((s32[]{:T(128)}, ...), condition=%wide.region_17.18_spmd, body=%wide.region_14.17_spmd.sunk | while | flops 630266880 | bytes 33242748 | solution.py:61
  362.2 31.0 %all_to_all.96 = bf16[2048,2,72]{2,1,0:T(2,128)(2,1)} all-to-all(bf16[2048,2,72]{2,1,0:T(2,128)(2,1)} %bitcast.405), channel_id=1, replica_groups=mesh['dp'=4,'sp'=8] {'sp'}, dimensions={0} | all-to-all | bytes 1179648 | tf_op jit(solution)/shard_map/all_to_all | solution.py:184
  426.1 9.0 fusion.78
  435.1 8.2 multiply_reduce_fusion.5
  494.1 16.0 all-to-all-done.4
  512.6 99.7 %while.39 = (s32[]{:T(128)}, f32[2048,2,72]{0,2,1:T(8,128)S(1)}, f32[2048,2,72]{0,2,1:T(8,128)}, bf16[4,512,2,72]{1,3,2,0:T(8,128)(2,1)}, bf16[4,512,2,72]{1,3,2...) while((s32[]{:T(128)}, f32[2048,2,72]{0,2,1:T(8,128)S(1)}, ...), condition=%wide.region_27.28_spmd.clone, body=%wide.region_25.27_spmd.clone.sunk | while | flops 1544002560 | bytes 143995632 | solution.py:113
  621.6 103.2 %all_to_all.97 = bf16[2048,3,2,72]{3,2,1,0:T(2,128)(2,1)} all-to-all(bf16[2048,3,2,72]{3,2,1,0:T(2,128)(2,1)} %copy.186), channel_id=1, replica_groups=mesh['dp'=4,'sp'=8] {'sp'}, dimensions={0} | all-to-all | bytes 3538944 | tf_op jit(solution)/shard_map/all_to_all | solution.py:312
  731.7 7.9 fusion.170
  740.7 12.2 fusion.169
  753.9 13.1 fusion.148
  774.9 41.7 %reduce-scatter.33.cloned.1.call-done = f32[1152,288]{0,1:T(8,128)} async-done(((f32[1152,2304]{0,1:T(8,128)}), f32[1152,288]{0,1:T(8,128)}) %reduce-scatter.33.cloned.1.call-update) | async-done | bytes 1327120 | tf_op jit(solution)/shard_map/reduce_scatter | solution.py:337
  819.7 160.7 %reduce-scatter.27.cloned.1.call-done = f32[1152,432]{0,1:T(8,128)} async-done(((f32[1152,3456]{0,1:T(8,128)}), f32[1152,432]{0,1:T(8,128)}) %reduce-scatter.27.cloned.1.call-update) | async-done | bytes 1990672 | tf_op jit(solution)/shard_map/reduce_scatter | solution.py:334
  983.6 207.6 %reduce-scatter.37.cloned.1.call-done = f32[1152,576]{0,1:T(8,128)} async-done(((f32[1152,4608]{0,1:T(8,128)}), f32[1152,576]{0,1:T(8,128)}) %reduce-scatter.37.cloned.1.call-update) | async-done | bytes 2654224 | tf_op jit(solution)/shard_map/reduce_scatter | solution.py:339
  1205.0 197.2 %reduce-scatter.39.cloned.1.call-done = f32[4608,144]{0,1:T(8,128)} async-done(((f32[4608,1152]{0,1:T(8,128)}), f32[4608,144]{0,1:T(8,128)}) %reduce-scatter.39.cloned.1.call-update) | async-done | bytes 2654224 | tf_op jit(solution)/shard_map/reduce_scatter | solution.py:340
  1408.8 10.2 fusion.90
  1422.8 26.0 %all-reduce = f32[6912]{0:T(1024)S(1)} all-reduce(f32[6912]{0:T(1024)S(1)} %reshape.342), channel_id=2, replica_groups=mesh['dp'=4,'sp'=8] {'sp'}, use_global_device_ids=true, to_apply=%region_31.32.clone | all-reduce | flops 6912 | bytes 55296
  1448.8 9.9 all-reduce.1
  1467.4 27.5 %reduce-scatter.51.cloned.1.call-done = f32[288,144]{1,0:T(8,128)} async-done(((f32[1152,144]{1,0:T(8,128)}), f32[288,144]{1,0:T(8,128)}) %reduce-scatter.51.cloned.1.call-update) | async-done | bytes 165904
  1496.7 34.4 %reduce-scatter.49.cloned.1.call-done = f32[288,288]{1,0:T(8,128)} async-done(((f32[1152,288]{1,0:T(8,128)}), f32[288,288]{1,0:T(8,128)}) %reduce-scatter.49.cloned.1.call-update) | async-done | bytes 331792
  1531.0 40.9 %reduce-scatter.43.cloned.1.call-done = f32[288,432]{1,0:T(8,128)} async-done(((f32[1152,432]{1,0:T(8,128)}), f32[288,432]{1,0:T(8,128)}) %reduce-scatter.43.cloned.1.call-update) | async-done | bytes 497680
  1571.9 46.0 %reduce-scatter.53.cloned.1.call-done = f32[288,576]{1,0:T(8,128)} async-done(((f32[1152,576]{1,0:T(8,128)}), f32[288,576]{1,0:T(8,128)}) %reduce-scatter.53.cloned.1.call-update) | async-done | bytes 663568
  1617.9 43.7 %reduce-scatter.41.cloned.1.call-done = f32[1152,144]{0,1:T(8,128)} async-done(((f32[4608,144]{0,1:T(8,128)}), f32[1152,144]{0,1:T(8,128)}) %reduce-scatter.41.cloned.1.call-update) | async-done | bytes 663568 | tf_op jit(solution)/shard_map/reduce_scatter | solution.py:350
  (392 shorter events, 447.3 us)
Async XLA Ops:
  7.2 201.9 %copy-start = (bf16[1152,1152]{1,0:T(8,128)(2,1)S(1)}, bf16[1152,1152]{1,0:T(8,128)(2,1)}, u32[]{:S(2)}) copy-start(bf16[1152,1152]{1,0:T(8,128)(2,1)} %param.28) | copy-start | bytes 7962628
  15.7 8.1 copy-start.9
  15.7 8.6 copy-start.47
  41.7 48.7 %all-to-all-start = ((bf16[256,3,16,72]{0,3,1,2:T(8,128)(2,1)}), bf16[256,3,16,72]{0,3,1,2:T(8,128)(2,1)}, u32[]{:S(2)}, u32[]{:S(2)}) async-start(bf16[256,3,16,72]{0,3,1,2:T(8,128)(2,1)} %copy.161), calls=%async_computation | async-start | bytes 3538944 | tf_op jit(solution)/shard_map/all_to_all | solution.py:182
  170.1 30.8 %all-to-all-start.1 = ((bf16[2048,2,72]{2,1,0:T(2,128)(2,1)}), bf16[2048,2,72]{2,1,0:T(2,128)(2,1)}, u32[]{:S(2)}, u32[]{:S(2)}) async-start(bf16[2048,2,72]{2,1,0:T(2,128)(2,1)} %bitcast.404), calls=%async_computation.1 | async-start | bytes 2097152 | tf_op jit(solution)/shard_map/all_to_all | solution.py:184
  256.1 46.4 %all-to-all-start.2 = ((bf16[256,3,16,72]{0,3,1,2:T(8,128)(2,1)}), bf16[256,3,16,72]{0,3,1,2:T(8,128)(2,1)}, u32[]{:S(2)}, u32[]{:S(2)}) async-start(bf16[256,3,16,72]{0,3,1,2:T(8,128)(2,1)} %copy.172), calls=%async_computation.2 | async-start | bytes 3538944 | tf_op jit(solution)/shard_map/all_to_all | solution.py:182
  260.5 506.6 %reduce-scatter.31.cloned.1.call-start = ((), (), s32[]{:S(2)}) async-start(), calls=%async_computation.22 | async-start | bytes 5971968 | tf_op jit(solution)/shard_map/reduce_scatter | solution.py:336
  416.4 26.9 %copy-start.5 = (f32[256,1152]{1,0:T(8,128)}, f32[256,1152]{1,0:T(8,128)S(1)}, u32[]{:S(2)}) copy-start(f32[256,1152]{1,0:T(8,128)S(1)} %get-tuple-element.462) | copy-start | bytes 3538948
  416.4 26.9 %copy-start.48 = (f32[256]{0:T(256)}, f32[256]{0:T(256)S(1)}, u32[]{:S(2)}) copy-start(f32[256]{0:T(256)S(1)} %broadcast_multiply_fusion) | copy-start | bytes 3076
  416.7 26.6 %copy-start.54 = (f32[256]{0:T(256)}, f32[256]{0:T(256)S(1)}, u32[]{:S(2)}) copy-start(f32[256]{0:T(256)S(1)} %fusion.138) | copy-start | bytes 3076
  417.9 8.2 copy-start.26
  458.8 310.9 %reduce-scatter.29.cloned.1.call-start = ((), (), s32[]{:S(2)}) async-start(), calls=%async_computation.21 | async-start | bytes 5971968 | tf_op jit(solution)/shard_map/reduce_scatter | solution.py:335
  467.9 304.4 %reduce-scatter.35.cloned.1.call-start = ((), (), s32[]{:S(2)}) async-start(), calls=%async_computation.24 | async-start | bytes 5971968 | tf_op jit(solution)/shard_map/reduce_scatter | solution.py:338
  477.0 8.2 copy-start.53
  479.3 30.8 %all-to-all-start.4 = ((bf16[256,16,72]{0,2,1:T(8,128)(2,1)}), bf16[256,16,72]{0,2,1:T(8,128)(2,1)}, u32[]{:S(2)}, u32[]{:S(2)}) async-start(bf16[256,16,72]{0,2,1:T(8,128)(2,1)} %bitcast.411), calls=%async_computation.4 | async-start | bytes 1179648 | tf_op jit(solution)/shard_map/all_to_all | solution.py:307
  483.5 333.1 %reduce-scatter.33.cloned.1.call-start = ((), (), s32[]{:S(2)}) async-start(), calls=%async_computation.23 | async-start | bytes 11943936 | tf_op jit(solution)/shard_map/reduce_scatter | solution.py:337
  494.1 486.3 %reduce-scatter.27.cloned.1.call-start = ((), (), s32[]{:S(2)}) async-start(), calls=%async_computation.20 | async-start | bytes 17915904 | tf_op jit(solution)/shard_map/reduce_scatter | solution.py:334
  549.0 8.1 copy-start.3
  574.1 8.1 copy-start.3
  739.6 451.5 %reduce-scatter.37.cloned.1.call-start = ((), (), s32[]{:S(2)}) async-start(), calls=%async_computation.25 | async-start | bytes 23887872 | tf_op jit(solution)/shard_map/reduce_scatter | solution.py:339
  752.9 649.3 %reduce-scatter.39.cloned.1.call-start = ((), (), s32[]{:S(2)}) async-start(), calls=%async_computation.26 | async-start | bytes 23887872 | tf_op jit(solution)/shard_map/reduce_scatter | solution.py:340
  767.0 696.8 %reduce-scatter.47.cloned.1.call-start = ((), (), s32[]{:S(2)}) async-start(), calls=%async_computation.30 | async-start | bytes 1474560
  769.6 696.0 %reduce-scatter.45.cloned.1.call-start = ((), (), s32[]{:S(2)}) async-start(), calls=%async_computation.29 | async-start | bytes 1474560
  772.2 722.6 %reduce-scatter.51.cloned.1.call-start = ((), (), s32[]{:S(2)}) async-start(), calls=%async_computation.32 | async-start | bytes 1474560
  774.8 756.2 %reduce-scatter.49.cloned.1.call-start = ((), (), s32[]{:S(2)}) async-start(), calls=%async_computation.31 | async-start | bytes 2211840
  819.7 752.2 %reduce-scatter.43.cloned.1.call-start = ((), (), s32[]{:S(2)}) async-start(), calls=%async_computation.28 | async-start | bytes 2949120
  983.5 634.3 %reduce-scatter.53.cloned.1.call-start = ((), (), s32[]{:S(2)}) async-start(), calls=%async_computation.33 | async-start | bytes 3686400
  1194.7 466.8 %reduce-scatter.41.cloned.1.call-start = ((), (), s32[]{:S(2)}) async-start(), calls=%async_computation.27 | async-start | bytes 3317760 | tf_op jit(solution)/shard_map/reduce_scatter | solution.py:350
  1205.0 198.4 %copy-start.13 = (f32[256,1152]{1,0:T(8,128)}, f32[256,1152]{1,0:T(8,128)S(1)}, u32[]{:S(2)}) copy-start(f32[256,1152]{1,0:T(8,128)S(1)} %get-tuple-element.470) | copy-start | bytes 3538948
  1419.0 40.3 %copy-start.61 = (f32[256]{0:T(256)S(1)}, f32[256]{0:T(256)}, u32[]{:S(2)}) copy-start(f32[256]{0:T(256)} %copy-done.60) | copy-start | bytes 3076
  1419.0 40.4 %copy-start.14 = (f32[256,1152]{1,0:T(8,128)S(1)}, f32[256,1152]{1,0:T(8,128)}, u32[]{:S(2)}) copy-start(f32[256,1152]{1,0:T(8,128)} %copy-done.13) | copy-start | bytes 3538948
  1461.1 200.4 %copy-start.1 = (bf16[1152,1152]{1,0:T(8,128)(2,1)S(1)}, bf16[1152,1152]{1,0:T(8,128)(2,1)}, u32[]{:S(2)}) copy-start(bf16[1152,1152]{1,0:T(8,128)(2,1)} %param.28) | copy-start | bytes 7962628
  (66 other events, 207.8 us)
Sparse Core Ops, SparseCore 0:
  458.9 68.9 reduce-scatter.30
  530.2 61.1 reduce-scatter.28
  593.6 79.3 reduce-scatter.34
  675.2 141.3 reduce-scatter.32
  818.9 161.4 reduce-scatter.26
  982.6 208.5 reduce-scatter.36
  1193.6 208.5 reduce-scatter.38
  1405.1 26.8 reduce-scatter.46
  1435.0 28.5 reduce-scatter.44
  1466.3 28.5 reduce-scatter.50
  1498.5 32.4 reduce-scatter.48
  1534.5 37.3 reduce-scatter.42
  1575.5 42.2 reduce-scatter.52
  1621.4 40.1 reduce-scatter.40
where the time goes:
time: 1680 us; the launch traced here: 1670 us
  waiting for transfers between devices  918 us (55%)
  matrix products  330 us (20%)
  blocking collectives  170 us (10%)
  local copies, waits for them, and re-layouts  147 us (9%)
  other arithmetic  66.9 us (4%)
  starting transfers between devices  20.2 us (1%)
    reduce_scatter x1, waiting for transfers between devices, local(): lax.psum_scatter(grad_up, 'sp', scatter_dimension=1, tiled=True)  208 us
    reduce_scatter x1, waiting for transfers between devices, local(): lax.psum_scatter(grad_down, 'sp', scatter_dimension=1, tiled=True)  197 us
    reduce_scatter x1, waiting for transfers between devices, local(): lax.psum_scatter(grad_qkv, 'sp', scatter_dimension=1, tiled=True)  161 us
    unnamed x20, waiting for transfers between devices  149 us
    all_to_all x1, blocking collectives, local(): lax.all_to_all(grad_proj, 'sp', split_axis=0, concat_axis=2, tiled=True)  103 us
    all_to_all x2, waiting for transfers between devices, forward(): lax.all_to_all(projected, 'sp', split_axis=2, concat_axis=0, tiled=True)  84.1 us
    dot_general x12, matrix products, matmul(): return jnp.dot(left, right, preferred_element_type=jnp.float32)  63.8 us
    unnamed x144, local copies, waits for them, and re-layouts  49 us
  transfers between devices with their start and end apart: 18, of which 13 were waited for; matrix products, arithmetic and copies ran while one was open for 15% of the time, Pallas kernels for 0%

commit v1 on v0

v1 whole, which is shorter than its diff:
```python
import functools
import math

import jax
import jax.numpy as jnp
from jax import lax
from jax.experimental import pallas as pl
from jax.experimental.pallas import tpu as pltpu
from jax.sharding import PartitionSpec as P

HEADS = 16
BIG = 1024
EPS = 1e-06
BIGNEG = -1e30
LOG2E = 1.4426950408889634
BF = jnp.bfloat16
F32 = jnp.float32
WIN = 256
VMEM_LIMIT = 48 * 1024 * 1024


def matmul(left, right):
    return jnp.dot(left, right, preferred_element_type=F32)


def matmul_tn(left, right):
    return lax.dot_general(left, right, (((0,), (0,)), ((), ())), preferred_element_type=F32)


def matmul_nt(left, right):
    return lax.dot_general(left, right, (((1,), (1,)), ((), ())), preferred_element_type=F32)


def head_window(head, width):
    size = width // HEADS
    low = head * size
    start = pl.multiple_of(jnp.minimum(low // 128 * 128, width - WIN), 128)
    lane = lax.broadcasted_iota(jnp.int32, (1, WIN), 1) + start
    mask = jnp.logical_and(lane >= low, lane < low + size)
    return pl.ds(start, WIN), mask


def keep_columns(ref, win, mask, value):
    ref[:, win] = jnp.where(mask, value, ref[:, win])


def attend_kernel(big_ref, q_ref, k0_ref, v0_ref, k1_ref, v1_ref, out_ref, lse_ref, *, factor):
    width = q_ref.shape[1]
    scale = factor * LOG2E

    def run(pairs):
        def one_head(head, carry):
            win, mask = head_window(head, width)
            query = q_ref[:, win] * mask.astype(BF)
            scores = [matmul_nt(query, key[:, win]) for key, _ in pairs]
            top = functools.reduce(jnp.maximum, [jnp.max(s, axis=1, keepdims=True) for s in scores])
            raised = [jnp.exp2((s - top) * scale) for s in scores]
            total = sum(jnp.sum(r, axis=1, keepdims=True) for r in raised)
            inverse = 1.0 / total
            result = sum(
                matmul((r * inverse).astype(BF), value[:, win])
                for r, (_, value) in zip(raised, pairs)
            )
            keep_columns(out_ref, win, mask, result.astype(BF))
            lane = lax.broadcasted_iota(jnp.int32, (1, 128), 1)
            lse = top * scale + jnp.log2(total)
            lse_ref[...] = jnp.where(lane == head, lse, lse_ref[...])
            return carry

        lax.fori_loop(0, HEADS, one_head, 0, unroll=2)

    lse_ref[...] = jnp.zeros_like(lse_ref)

    @pl.when(big_ref[0] == 1)
    def _():
        run([(k0_ref, v0_ref), (k1_ref, v1_ref)])

    @pl.when(big_ref[0] == 0)
    def _():
        run([(k0_ref, v0_ref)])


def query_grad_kernel(
    big_ref, q_ref, k0_ref, v0_ref, k1_ref, v1_ref, do_ref, stat_ref, out_ref, *, factor
):
    width = q_ref.shape[1]
    scale = factor * LOG2E

    def run(pairs):
        def one_head(head, carry):
            win, mask = head_window(head, width)
            keep = mask.astype(BF)
            query = q_ref[:, win] * keep
            grad = do_ref[:, win] * keep
            lane = lax.broadcasted_iota(jnp.int32, (1, 128), 1)
            stat = stat_ref[...]
            lse = jnp.sum(jnp.where(lane == head, stat, 0.0), axis=1, keepdims=True)
            delta = jnp.sum(jnp.where(lane == head + HEADS, stat, 0.0), axis=1, keepdims=True)
            total = None
            for key, value in pairs:
                prob = jnp.exp2(matmul_nt(query, key[:, win]) * scale - lse)
                grad_prob = matmul_nt(grad, value[:, win])
                grad_score = (prob * (grad_prob - delta)).astype(BF)
                part = matmul(grad_score, key[:, win])
                total = part if total is None else total + part
            keep_columns(out_ref, win, mask, (total * factor).astype(BF))
            return carry

        lax.fori_loop(0, HEADS, one_head, 0, unroll=2)

    @pl.when(big_ref[0] == 1)
    def _():
        run([(k0_ref, v0_ref), (k1_ref, v1_ref)])

    @pl.when(big_ref[0] == 0)
    def _():
        run([(k0_ref, v0_ref)])


def key_grad_kernel(
    big_ref, k_ref, v_ref, q0_ref, q1_ref, pack0_ref, pack1_ref, dk_ref, dv_ref, stats, *, factor
):
    width = k_ref.shape[1]
    rows = k_ref.shape[0]
    scale = factor * LOG2E
    blocks = 1 + pack1_ref.shape[0]

    def unpack(block, pack):
        both = pack[rows : rows + 16, :].astype(F32)
        joined = both[:8] + both[8:]
        for group in range(4):
            stats[block, 8 * group : 8 * group + 8, :] = joined[:, group * rows : group * rows + rows]

    unpack(0, pack0_ref[...])
    for block in range(1, blocks):
        unpack(block, pack1_ref[block - 1])

    def run(count):
        def one_head(head, carry):
            win, mask = head_window(head, width)
            keep = mask.astype(BF)
            key = k_ref[:, win] * keep
            value = v_ref[:, win] * keep
            grad_key = grad_value = None
            for block in range(count):
                if block == 0:
                    query, grad = q0_ref[:, win], pack0_ref[0:rows, win]
                else:
                    query = q1_ref[(block - 1) * rows : block * rows, win]
                    grad = pack1_ref[block - 1, 0:rows, win]
                lse = stats[block, pl.ds(head, 1), :]
                delta = stats[block, pl.ds(head + HEADS, 1), :]
                prob = jnp.exp2(matmul_nt(key, query) * scale - lse)
                grad_prob = matmul_nt(value, grad)
                grad_score = (prob * (grad_prob - delta)).astype(BF)
                part_value = matmul(prob.astype(BF), grad)
                part_key = matmul(grad_score, query)
                grad_value = part_value if block == 0 else grad_value + part_value
                grad_key = part_key if block == 0 else grad_key + part_key
            keep_columns(dk_ref, win, mask, (grad_key * factor).astype(BF))
            keep_columns(dv_ref, win, mask, grad_value.astype(BF))
            return carry

        lax.fori_loop(0, HEADS, one_head, 0, unroll=2)

    @pl.when(big_ref[0] == 1)
    def _():
        run(blocks)

    @pl.when(big_ref[0] == 0)
    def _():
        run(1)


def text_probs(query, key, scale, live):
    scores = matmul_nt(query, key)
    lane = lax.broadcasted_iota(jnp.int32, (1, scores.shape[1]), 1)
    scores = jnp.where(lane < live, scores, BIGNEG)
    raised = jnp.exp2((scores - jnp.max(scores, axis=1, keepdims=True)) * scale)
    return raised * (1.0 / jnp.sum(raised, axis=1, keepdims=True))


def cross_kernel(q_ref, k_ref, v_ref, out_ref, *, factor, live):
    width = q_ref.shape[1]

    def one_head(head, carry):
        win, mask = head_window(head, width)
        query = q_ref[:, win] * mask.astype(BF)
        probs = text_probs(query, k_ref[:, win], factor * LOG2E, live)
        keep_columns(out_ref, win, mask, matmul(probs.astype(BF), v_ref[:, win]).astype(BF))
        return carry

    lax.fori_loop(0, HEADS, one_head, 0, unroll=4)


def cross_grad_kernel(q_ref, g_ref, k_ref, v_ref, dq_ref, dk_ref, dv_ref, *, factor, live):
    width = q_ref.shape[1]

    def one_head(head, carry):
        win, mask = head_window(head, width)
        keep = mask.astype(BF)
        query = q_ref[:, win]
        grad = g_ref[:, win]
        key = k_ref[:, win]
        probs = text_probs(query * keep, key, factor * LOG2E, live)
        grad_probs = matmul_nt(grad * keep, v_ref[:, win])
        inner = jnp.sum(probs * grad_probs, axis=1, keepdims=True)
        grad_scores = (probs * (grad_probs - inner)).astype(BF)
        keep_columns(dq_ref, win, mask, (matmul(grad_scores, key) * factor).astype(BF))
        keep_columns(dk_ref, win, mask, matmul_tn(grad_scores, query) * factor)
        keep_columns(dv_ref, win, mask, matmul_tn(probs.astype(BF), grad))
        return carry

    lax.fori_loop(0, HEADS, one_head, 0, unroll=4)


def weight_grad_kernel(x0_ref, x1_ref, g0_ref, g1_ref, out_ref, turned):
    rows, width = x0_ref.shape
    step = pl.program_id(0)

    @pl.when(step == 0)
    def _():
        for part, ref in enumerate((x0_ref, x1_ref)):
            for low in range(0, width, 128):
                turned[low : low + 128, part * rows : part * rows + rows] = ref[:, low : low + 128].T

    tall = out_ref.shape[0]
    here = pl.ds(pl.multiple_of(step * tall, 16), tall)
    total = matmul(turned[here, 0:rows], g0_ref[...]) + matmul(turned[here, rows:], g1_ref[...])
    out_ref[...] = total.astype(out_ref.dtype)


def whole(shape):
    return pl.BlockSpec(shape, lambda *_: (0,) * len(shape))


def params():
    return pltpu.CompilerParams(vmem_limit_bytes=VMEM_LIMIT)


def cost(flops, nbytes, exps=0):
    return pl.CostEstimate(flops=int(flops), bytes_accessed=int(nbytes), transcendentals=int(exps))


def part_spec(rows, width, at):
    return pl.BlockSpec((rows, width), lambda i, *_: (0, at))


def attend(big, own, others, factor):
    rows, width = own.shape[0], own.shape[1] // 3
    far = others.shape[0]
    return pl.pallas_call(
        functools.partial(attend_kernel, factor=factor),
        grid_spec=pltpu.PrefetchScalarGridSpec(
            num_scalar_prefetch=1,
            grid=(1,),
            in_specs=[
                part_spec(rows, width, 0),
                part_spec(rows, width, 1),
                part_spec(rows, width, 2),
                part_spec(far, width, 1),
                part_spec(far, width, 2),
            ],
            out_specs=[whole((rows, width)), whole((rows, 128))],
        ),
        out_shape=[
            jax.ShapeDtypeStruct((rows, width), BF),
            jax.ShapeDtypeStruct((rows, 128), F32),
        ],
        compiler_params=params(),
        cost_estimate=cost(4 * HEADS * rows * (rows + far) * WIN, 6 * far * width, HEADS * rows * far),
    )(big, own, own, own, others, others)


def query_grad(big, own, others, grad, stat, factor):
    rows, width = own.shape[0], own.shape[1] // 3
    far = others.shape[0]
    return pl.pallas_call(
        functools.partial(query_grad_kernel, factor=factor),
        grid_spec=pltpu.PrefetchScalarGridSpec(
            num_scalar_prefetch=1,
            grid=(1,),
            in_specs=[
                part_spec(rows, width, 0),
                part_spec(rows, width, 1),
                part_spec(rows, width, 2),
                part_spec(far, width, 1),
                part_spec(far, width, 2),
                whole((rows, width)),
                whole((rows, 128)),
            ],
            out_specs=whole((rows, width)),
        ),
        out_shape=jax.ShapeDtypeStruct((rows, width), BF),
        compiler_params=params(),
        cost_estimate=cost(6 * HEADS * rows * (rows + far) * WIN, 6 * far * width, HEADS * rows * far),
    )(big, own, own, own, others, others, grad, stat)


def key_grad(big, own, others, pack, packs, factor):
    rows, width = own.shape[0], own.shape[1] // 3
    far = others.shape[0]
    return pl.pallas_call(
        functools.partial(key_grad_kernel, factor=factor),
        grid_spec=pltpu.PrefetchScalarGridSpec(
            num_scalar_prefetch=1,
            grid=(1,),
            in_specs=[
                part_spec(rows, width, 1),
                part_spec(rows, width, 2),
                part_spec(rows, width, 0),
                part_spec(far, width, 0),
                whole(pack.shape),
                whole(packs.shape),
            ],
            out_specs=[whole((rows, width))] * 2,
            scratch_shapes=[pltpu.VMEM((1 + packs.shape[0], 2 * HEADS, rows), F32)],
        ),
        out_shape=[jax.ShapeDtypeStruct((rows, width), BF)] * 2,
        compiler_params=params(),
        cost_estimate=cost(8 * HEADS * rows * (rows + far) * WIN, 6 * far * width, HEADS * rows * far),
    )(big, own, own, own, others, pack, packs)


def cross_attend(queries, keys, values, factor, live):
    rows, width = queries.shape
    return pl.pallas_call(
        functools.partial(cross_kernel, factor=factor, live=live),
        out_shape=jax.ShapeDtypeStruct((rows, width), BF),
        compiler_params=params(),
        cost_estimate=cost(4 * HEADS * rows * 128 * WIN, 6 * rows * width, HEADS * rows * 128),
    )(queries, keys, values)


def cross_grad(queries, grad, keys, values, factor, live):
    rows, width = queries.shape
    return pl.pallas_call(
        functools.partial(cross_grad_kernel, factor=factor, live=live),
        out_shape=[
            jax.ShapeDtypeStruct((rows, width), BF),
            jax.ShapeDtypeStruct(keys.shape, F32),
            jax.ShapeDtypeStruct(keys.shape, F32),
        ],
        compiler_params=params(),
        cost_estimate=cost(10 * HEADS * rows * 128 * WIN, 12 * rows * width, HEADS * rows * 128),
    )(queries, grad, keys, values)


def weight_grad(x0, x1, g0, g1):
    rows, width = x0.shape
    depth = g0.shape[1]
    tall = width // 4
    return pl.pallas_call(
        weight_grad_kernel,
        grid=(4,),
        in_specs=[whole((rows, width))] * 2 + [whole((rows, depth))] * 2,
        out_specs=pl.BlockSpec((tall, depth), lambda i: (i, 0)),
        out_shape=jax.ShapeDtypeStruct((width, depth), BF),
        scratch_shapes=[pltpu.VMEM((width, 2 * rows), BF)],
        compiler_params=params(),
        cost_estimate=cost(4 * rows * width * depth, 2 * width * depth + 4 * rows * (width + depth)),
    )(x0, x1, g0, g1)


def normal(stream):
    centred = stream - jnp.mean(stream, axis=-1, keepdims=True)
    spread = lax.rsqrt(jnp.mean(centred * centred, axis=-1, keepdims=True) + EPS)
    return centred * spread, spread


def norm_back(normed, spread, scale, grad):
    scaled = grad * (1.0 + scale)
    back = spread * (
        scaled
        - jnp.mean(scaled, axis=-1, keepdims=True)
        - normed * jnp.mean(scaled * normed, axis=-1, keepdims=True)
    )
    return back, jnp.sum(grad, axis=0), jnp.sum(grad * normed, axis=0)


def local(
    tokens,
    image_len,
    timestep,
    caption,
    time_embed,
    mod_table,
    w_qkv,
    w_out,
    cross_q,
    cross_kv,
    cross_out,
    w_up,
    w_down,
    cotangent,
):
    sp_count = lax.axis_size("sp")
    dp_count = lax.axis_size("dp")
    place = lax.axis_index("sp")
    core = place % 2
    stream_in = tokens[0].astype(F32)
    rows, width = stream_in.shape
    factor = 1.0 / math.sqrt(width // HEADS)
    blocks = BIG // rows

    ends = jnp.cumsum(image_len[0])
    label = jnp.sum((ends <= place * rows).astype(jnp.int32))
    length = image_len[0, label]
    within = place - (ends[label] - length) // rows
    large = (length > rows).astype(jnp.int32)
    big = large.reshape(1)
    modulation = lax.dynamic_slice_in_dim(time_embed, timestep[0, label], 1, axis=0).reshape(6, width) + mod_table
    shift_one, scale_one, gate_one, shift_two, scale_two, gate_two = [modulation[i] for i in range(6)]

    to_right = [(i, i + 1) for i in range(sp_count - 1)]
    to_left = [(i + 1, i) for i in range(sp_count - 1)]
    to_pair = [(i, i ^ 1) for i in range(sp_count)]

    def image_blocks(block):
        from_left, from_right = [block], [block]
        for _ in range(blocks - 1):
            from_left.append(lax.ppermute(from_left[-1], "sp", to_right))
            from_right.append(lax.ppermute(from_right[-1], "sp", to_left))
        return [
            jnp.where(within + i < blocks, from_right[i], from_left[blocks - i])
            for i in range(1, blocks)
        ]

    normed_one, spread_one = normal(stream_in)
    first_in = (normed_one * (1.0 + scale_one) + shift_one).astype(BF)
    other_in = jnp.concatenate(image_blocks(first_in), axis=0)

    def halves(grad):
        count = sp_count
        size = grad.shape[1] // count
        even, odd = [
            jnp.concatenate([grad[:, i * size : (i + 1) * size] for i in range(c, count, 2)], axis=1)
            for c in (0, 1)
        ]
        first = core == 0
        return jnp.where(first, even, odd), jnp.where(first, odd, even)

    def pair_grad(acts, grad):
        keep, send = halves(grad)
        return weight_grad(acts, lax.ppermute(acts, "sp", to_pair), keep, lax.ppermute(send, "sp", to_pair))

    groups = [[c + 2 * z for z in range(sp_count // 2)] for c in (0, 1)]

    def spread_sum(part):
        part = lax.psum_scatter(part, "dp", scatter_dimension=0, tiled=True)
        return lax.psum_scatter(
            part, "sp", scatter_dimension=1, axis_index_groups=groups, tiled=True
        ).astype(F32)

    caption_rows = caption[0]
    live = caption_rows.shape[0]
    padded = -(-live // 128) * 128
    caption_pad = jnp.concatenate([caption_rows, jnp.zeros((padded - live, width), BF)], axis=0)
    text_kv = matmul(caption_pad, cross_kv).astype(BF)
    text_keys, text_values = text_kv[:, :width], text_kv[:, width:]
    own = matmul(first_in, w_qkv).astype(BF)
    others = matmul(other_in, w_qkv).astype(BF)
    attended, logsum = attend(big, own, others, factor)
    attn_branch = matmul(attended, w_out)
    stream_one = stream_in + gate_one * attn_branch
    cross_in = stream_one.astype(BF)
    cross_queries = matmul(cross_in, cross_q).astype(BF)
    cross_mixed = cross_attend(cross_queries, text_keys, text_values, factor, live)
    stream_two = stream_one + matmul(cross_mixed, cross_out)
    normed_two, spread_two = normal(stream_two)
    second_in = (normed_two * (1.0 + scale_two) + shift_two).astype(BF)
    hidden_pre = matmul(second_in, w_up)
    angle = math.sqrt(2.0 / math.pi) * (hidden_pre + 0.044715 * hidden_pre * hidden_pre * hidden_pre)
    bend = jnp.tanh(angle)
    hidden = (0.5 * hidden_pre * (1.0 + bend)).astype(BF)
    mlp_branch = matmul(hidden, w_down)
    stream_three = stream_two + gate_two * mlp_branch

    grad_three = cotangent[0].astype(F32)
    grad_gate_two = jnp.sum(grad_three * mlp_branch, axis=0)
    grad_mlp = (gate_two * grad_three).astype(BF)
    part_down = pair_grad(hidden, grad_mlp)
    slope = 0.5 * (1.0 + bend) + 0.5 * hidden_pre * (1.0 - bend * bend) * math.sqrt(2.0 / math.pi) * (
        1.0 + 3 * 0.044715 * hidden_pre * hidden_pre
    )
    grad_pre = (matmul_nt(grad_mlp, w_down) * slope).astype(BF)
    part_up = pair_grad(second_in, grad_pre)
    grad_second = matmul_nt(grad_pre, w_up)
    back_two, grad_shift_two, grad_scale_two = norm_back(normed_two, spread_two, scale_two, grad_second)
    grad_stream_two = grad_three + back_two
    grad_cross = grad_stream_two.astype(BF)
    part_co = pair_grad(cross_mixed, grad_cross)
    grad_mixed = matmul_nt(grad_cross, cross_out).astype(BF)
    grad_cq_rows, grad_text_keys, grad_text_values = cross_grad(
        cross_queries, grad_mixed, text_keys, text_values, factor, live
    )
    grad_text = jnp.concatenate([grad_text_keys[:live], grad_text_values[:live]], axis=1)
    part_cq = pair_grad(cross_in, grad_cq_rows)
    grad_stream_one = grad_stream_two + matmul_nt(grad_cq_rows, cross_q)
    grad_gate_one = jnp.sum(grad_stream_one * attn_branch, axis=0)
    grad_attn = (gate_one * grad_stream_one).astype(BF)
    part_out = pair_grad(attended, grad_attn)
    grad_back = matmul_nt(grad_attn, w_out).astype(BF)

    column = jnp.arange(width, dtype=jnp.int32)[:, None] // (width // HEADS)
    pick = (column + HEADS == jnp.arange(128, dtype=jnp.int32)[None, :]).astype(F32)
    inner = jnp.dot(
        grad_back.astype(F32) * attended.astype(F32), pick, precision=lax.Precision.HIGHEST
    )
    stat = logsum + inner
    turned = stat.T[: 2 * HEADS].reshape(4, 8, rows).transpose(1, 0, 2).reshape(8, 4 * rows)
    high = lax.reduce_precision(turned, exponent_bits=8, mantissa_bits=7)
    both = jnp.concatenate([high, turned - high], axis=0).astype(BF)
    both = jnp.concatenate([both, jnp.zeros((16, width - 4 * rows), BF)], axis=1)
    pack = jnp.concatenate([grad_back, both], axis=0)
    packs = jnp.stack(image_blocks(pack))
    grad_queries = query_grad(big, own, others, grad_back, stat, factor)
    grad_keys, grad_values = key_grad(big, own, others, pack, packs, factor)
    grad_proj = jnp.concatenate([grad_queries, grad_keys, grad_values], axis=1)
    part_qkv = pair_grad(first_in, grad_proj)
    grad_first = matmul_nt(grad_proj, w_qkv)
    back_one, grad_shift_one, grad_scale_one = norm_back(normed_one, spread_one, scale_one, grad_first)
    grad_tokens = grad_stream_one + back_one

    final_down = spread_sum(part_down)
    final_up = spread_sum(part_up)
    final_co = spread_sum(part_co)
    final_cq = spread_sum(part_cq)
    final_out = spread_sum(part_out)
    final_qkv = spread_sum(part_qkv)
    text_part = lax.psum_scatter(grad_text, "sp", scatter_dimension=1, tiled=True).astype(BF)
    part_ckv = matmul_tn(caption_rows, text_part).astype(BF)
    final_ckv = lax.psum_scatter(part_ckv, "dp", scatter_dimension=0, tiled=True).astype(F32)
    table = jnp.concatenate(
        [grad_shift_one, grad_scale_one, grad_gate_one, grad_shift_two, grad_scale_two, grad_gate_two]
    )
    arranged = table.reshape(dp_count, sp_count, -1).transpose(1, 0, 2).reshape(-1)
    final_table = lax.psum_scatter(
        lax.psum_scatter(arranged, "sp", scatter_dimension=0, tiled=True),
        "dp",
        scatter_dimension=0,
        tiled=True,
    )
    return (
        stream_three[None],
        grad_tokens[None],
        final_table,
        final_qkv,
        final_out,
        final_cq,
        final_ckv,
        final_co,
        final_up,
        final_down,
    )


def solution(mesh):
    return jax.shard_map(
        local,
        mesh=mesh,
        in_specs=(
            P("dp", "sp", None),
            P("dp", None),
            P("dp", None),
            P("dp", None, None),
            P(),
            P(),
            P(),
            P(),
            P(),
            P(),
            P(),
            P(),
            P(),
            P("dp", "sp", None),
        ),
        out_specs=(
            P("dp", "sp", None),
            P("dp", "sp", None),
            P(("dp", "sp")),
            P("dp", "sp"),
            P("dp", "sp"),
            P("dp", "sp"),
            P("dp", "sp"),
            P("dp", "sp"),
            P("dp", "sp"),
            P("dp", "sp"),
        ),
        check_vma=False,
    )
```

time: 1680 us -> 696 us (0.41)
  waiting for transfers between devices: 918 us -> 323 us
  matrix products: 330 us -> 72.7 us
  blocking collectives: 170 us -> 37.4 us
  local copies, waits for them, and re-layouts: 147 us -> 61.1 us
  Pallas kernels: 0 us -> 66.4 us
  starting transfers between devices: 20.2 us -> 77.2 us
  other arithmetic: 66.9 us -> 24.1 us
    reduce_scatter x8 -> x6, waiting for transfers between devices: 651 us -> 174 us  [spread_sum(): part = lax.psum_scatter(part, 'dp', scatter_dimension=0, tiled=True)]
    dot_general x53 -> x9, matrix products: 214 us -> 42.9 us  [the longest x8 42.1 us: matmul(): return jnp.dot(left, right, preferred_element_type=F32)]
    all_to_all x2 -> x0, blocking collectives: 134 us -> none  [the longest x1 103 us: local(): lax.all_to_all(grad_proj, 'sp', split_axis=0, concat_axis=2, tiled=True)]
    all_to_all x4 -> x0, waiting for transfers between devices: 118 us -> none  [the longest x2 84.1 us: forward(): lax.all_to_all(projected, 'sp', split_axis=2, concat_axis=0, tiled=True)]
    ppermute x0 -> x24, starting transfers between devices: none -> 76.7 us  [the longest x6 32.2 us: image_blocks(): from_left.append(lax.ppermute(from_left[-1], 'sp', to_right))]
    pallas_call x0 -> x11, Pallas kernels: none -> 66.4 us  [the longest x6 28.4 us: weight_grad(): pl.pallas_call(weight_grad_kernel, grid=(4,), in_specs=[whole((rows, widt...]
    dot_general x6 -> x1, matrix products: 43.2 us -> 0.36 us  [matmul_tn(): lax.dot_general(left, right, (((0,), (0,)), ((), ())), preferred_element_...]
    sub x6 -> x0, matrix products: 38.3 us -> none  [the longest x4 31.8 us: one_block(): raised = jnp.exp(scores - row_max)]
  transfers between devices with their start and end apart: 18 -> 38, of which waited for: 13 -> 13; matrix products, arithmetic and copies ran while one was open for 15% -> 12% of each run, Pallas kernels for 0% -> 6%
where the time goes in v1:
time: 696 us; the launch traced here: 686 us
  waiting for transfers between devices  323 us (46%)
  starting transfers between devices  77.2 us (11%)
  matrix products  72.7 us (10%)
  Pallas kernels  66.4 us (10%)
  local copies, waits for them, and re-layouts  61.1 us (9%)
  blocking collectives  37.4 us (5%)
  other arithmetic  24.1 us (3%)
  between operations  24.1 us (3%)
    reduce_scatter x6, waiting for transfers between devices, spread_sum(): part = lax.psum_scatter(part, 'dp', scatter_dimension=0, tiled=True)  174 us
    unnamed x22, waiting for transfers between devices  139 us
    dot_general x8, matrix products, matmul(): return jnp.dot(left, right, preferred_element_type=F32)  42.1 us
    unnamed x166, local copies, waits for them, and re-layouts  41.5 us
    unnamed x2, blocking collectives  37.4 us
    ppermute x6, starting transfers between devices, image_blocks(): from_left.append(lax.ppermute(from_left[-1], 'sp', to_right))  32.2 us
    dot_general x6, matrix products, matmul_nt(): lax.dot_general(left, right, (((1,), (1,)), ((), ())), preferred_element_...  29.5 us
    pallas_call x6, Pallas kernels, weight_grad(): pl.pallas_call(weight_grad_kernel, grid=(4,), in_specs=[whole((rows, widt...  28.4 us
  transfers between devices with their start and end apart: 38, of which 13 were waited for; matrix products, arithmetic and copies ran while one was open for 12% of the time, Pallas kernels for 6%

profile of v1, /device:TPU:0, one launch (start us, length us, event | category | flops | bytes accessed | tf_op | source)
XLA Modules:
  0.0 686.1 jit_solution(5106349000009283188)
XLA Ops:
  25.1 7.1 %convolution_convert_fusion.1.q_ref.k0_ref.v0_ref.k_ref.v_ref.q0_ref = bf16[256,3456]{1,0:T(8,128)(2,1)} fusion(bf16[256,1152]{1,0:T(8,128)(2,1)S(1)} %fusion.27.x0_ref, bf16[1152,3456]{1,0:T(8,128)(2,1)} %param.20), kind=kOutput, calls=%fused_computation.5 | convolution fusion | flops 2039316480 | bytes 10321920 | tf_op jit(solution)/shard_map/dot_general | solution.py:23
  34.4 5.2 collective-permute-start.2
  47.2 7.3 %collective-permute-start.3 = (bf16[256,1152]{1,0:T(8,128)(2,1)}, bf16[256,1152]{1,0:T(8,128)(2,1)S(1)}, u32[]{:S(2)}, u32[]{:S(2)}) collective-permute-start(bf16[256,1152]{1,0:T(8,128)(2,1)} %collective-permute-done.2), channel_id=1, source_target_pairs={{0,1},{1,2},{2,3},{3,4},{4,5},{5,6},{6,7},{8,9},{9,10},{10,11},{11... | collective-permute-start | bytes 1769480 | tf_op jit(solution)/shard_map/ppermute | solution.py:422
  56.8 13.5 %convolution_convert_fusion.k1_ref.v1_ref.q1_ref = bf16[768,3456]{1,0:T(8,128)(2,1)} fusion(bf16[1152,3456]{1,0:T(8,128)(2,1)} %param.20, bf16[256,1152]{1,0:T(8,128)(2,1)S(1)} %broadcast_select_fusion.4, bf16[256,1152]{1,0:T(8,128)(2,1)S(1)} %broadcast_select_fusion.5, bf16[256,1152]{1,0:T(8,128)(2,1)S(1)} %broadcast_select_fusion.6), kind=kOutput, calls=%fused_computation.3 | convolution fusion | flops 6123257856 | bytes 15040512 | tf_op jit(solution)/shard_map/dot_general | solution.py:23
  70.3 9.8 %shard_map.213 = (bf16[256,1152]{1,0:T(8,128)(2,1)S(1)}, f32[256,128]{1,0:T(8,128)S(1)}) custom-call(s32[1]{0:T(128)} %bitcast.3.big_ref, bf16[256,3456]{1,0:T(8,128)(2,1)S(1)} %copy-done.2, bf16[256,3456]{1,0:T(8,128)(2,1)S(1)} %copy-done.2, bf16[256,3456]{1,0:T(8,128)(2,1)S(1)} %copy-done.2, ...), custom_call_target="tpu_custom_call" | custom-call | flops 4294967296 | bytes 5308416 | tf_op jit(solution)/shard_map/pallas_call | solution.py:252
  82.4 5.8 shard_map.214.x0_ref
  91.0 6.8 multiply_convert_fusion
  97.9 8.0 %fusion = bf16[256,4608]{1,0:T(8,128)(2,1)S(1)} fusion(bf16[256,1152]{1,0:T(8,128)(2,1)S(1)} %copy-done.34, bf16[4608,1152]{1,0:T(8,128)(2,1)} %param.26, f32[256,4608]{1,0:T(8,128)S(1)} %get-tuple-element.155), kind=kOutput, calls=%fused_computation.4 | convolution fusion | flops 2740322304 | bytes 18284544 | tf_op jit(solution)/shard_map/dot_general | solution.py:31
  105.9 8.9 %multiply_reduce_fusion = (f32[1152]{0:T(1024)}, f32[256]{0:T(256)S(1)}, f32[256]{0:T(256)S(1)}, f32[1152]{0:T(1024)}, f32[256,1152]{1,0:T(8,128)S(1)}) fusion(f32[256,1152]{1,0:T(8,128)S(1)} %get-tuple-element.153, f32[256]{0:T(256)S(1)} %add_rsqrt_fusion, f32[256]{0:T(256)S(1)} %broadcast_multiply_fusion.4, f32[1152]{0:T(1024)S(1)} %copy-done.53, ...), kind=kOutput, calls=%fused_computation.56 | convolution fusion | flops 2720560640 | bytes 15353344 | tf_op jit(solution)/shard_map/dot_general | solution.py:31
  114.8 9.6 %fusion.36 = (f32[1152]{0:T(1024)}, f32[1,256,1152]{2,1,0:T(8,128)}, bf16[256,1152]{1,0:T(8,128)(2,1)S(1)}, f32[256,1152]{1,0:T(8,128)}) fusion(bf16[1,256,1152]{2,1,0:T(8,128)(2,1)S(1)} %copy-done.50, f32[256,1152]{1,0:T(8,128)S(1)} %get-tuple-element.153, f32[1152]{0:T(1024)S(1)} %copy-done.52, f32[256]{0:T(256)S(1)} %broadcast_multiply_fusion.2, ...), kind=kOutput, calls=%fused_computation.55 | convolution fusion | flops 2722036736 | bytes 18892288 | tf_op jit(solution)/shard_map/dot_general | solution.py:23
  126.3 8.7 %shard_map.215 = (bf16[256,1152]{1,0:T(8,128)(2,1)S(1)}, f32[128,1152]{1,0:T(8,128)S(1)}, f32[128,1152]{1,0:T(8,128)S(1)}) custom-call(bf16[256,1152]{1,0:T(8,128)(2,1)S(1)} %convolution_convert_fusion.6.q_ref, bf16[256,1152]{1,0:T(8,128)(2,1)S(1)} %convolution_convert_fusion.5.g_ref, bf16[128,1152]{1,0:T(8,128)(2,1)S(1)} %copy-done.23, ...), custom_call_target="tpu_custom_call" | custom-call | flops 1342177280 | bytes 3538944 | tf_op jit(solution)/shard_map/pallas_call | solution.py:337
  139.7 6.6 collective-permute-start.14
  172.4 15.2 %collective-permute-start.18 = (bf16[256,1152]{1,0:T(8,128)(2,1)}, bf16[256,1152]{1,0:T(8,128)(2,1)S(1)}, u32[]{:S(2)}, u32[]{:S(2)}) collective-permute-start(bf16[256,1152]{1,0:T(8,128)(2,1)} %shard_map.214.x0_ref), channel_id=1, source_target_pairs={{0,1},{1,0},{2,3},{3,2},{4,5},{5,4},{6,7},{7,6},{8,9},{9,8},{10,11... | collective-permute-start | bytes 1769480 | tf_op jit(solution)/shard_map/ppermute | solution.py:445
  193.2 7.1 %shard_map.216 = bf16[256,1152]{1,0:T(8,128)(2,1)S(1)} custom-call(s32[1]{0:T(128)} %bitcast.3.big_ref, bf16[256,3456]{1,0:T(8,128)(2,1)S(1)} %copy-done.3, bf16[256,3456]{1,0:T(8,128)(2,1)S(1)} %copy-done.3, bf16[256,3456]{1,0:T(8,128)(2,1)S(1)} %copy-done.3, bf16[768,3456]{1,0:T(8,128)(2,1)} %convolution_convert_fusion.k1_ref.v1_ref.q1_ref, ...), custom_call_target="tpu_custom_call" | custom-call | flops 6442450944 | bytes 5308416 | tf_op jit(solution)/shard_map/pallas_call | solution.py:278
  200.3 4.4 shard_map.221
  204.8 8.6 %collective-permute-start.9 = (bf16[272,1152]{1,0:T(8,128)(2,1)}, bf16[272,1152]{1,0:T(8,128)(2,1)S(1)}, u32[]{:S(2)}, u32[]{:S(2)}) collective-permute-start(bf16[272,1152]{1,0:T(8,128)(2,1)} %collective-permute-done.8), channel_id=1, source_target_pairs={{0,1},{1,2},{2,3},{3,4},{4,5},{5,6},{6,7},{8,9},{9,10},{10,11},{11... | collective-permute-start | bytes 1880072 | tf_op jit(solution)/shard_map/ppermute | solution.py:422
  216.9 6.7 shard_map.217
  230.3 12.6 %collective-permute-start.13 = (bf16[256,1728]{0,1:T(8,128)(2,1)}, bf16[256,1728]{0,1:T(8,128)(2,1)}, u32[]{:S(2)}, u32[]{:S(2)}) collective-permute-start(bf16[256,1728]{0,1:T(8,128)(2,1)} %copy.53), channel_id=1, source_target_pairs={{0,1},{1,0},{2,3},{3,2},{4,5},{5,4},{6,7},{7,6},{8,9},{9,8},{10,11... | collective-permute-start | bytes 2654216 | tf_op jit(solution)/shard_map/ppermute | solution.py:445
  247.6 5.6 shard_map.218
  268.0 5.2 shard_map.222
  279.8 7.1 %shard_map.223 = bf16[4608,576]{1,0:T(8,128)(2,1)} custom-call(bf16[256,4608]{1,0:T(8,128)(2,1)S(1)} %copy-done.12, bf16[256,4608]{1,0:T(8,128)(2,1)S(1)} %collective-permute-done.22.x1_ref, bf16[256,576]{1,0:T(8,128)(2,1)S(1)} %get-tuple-element.99.g0_ref, bf16[256,576]{1,0:T(8,128)(2,1)S(1)} %collective-permute-done.23.g1_ref), custom_call_target="tpu_custom_call" | custom-call | flops 2717908992 | bytes 10616832 | tf_op jit(solution)/shard_map/pallas_call | solution.py:353
  295.9 43.5 %reduce-scatter.31.cloned.1.call-done = bf16[288,1728]{1,0:T(8,128)(2,1)} async-done(((bf16[1152,1728]{1,0:T(8,128)(2,1)}), bf16[288,1728]{1,0:T(8,128)(2,1)}) %reduce-scatter.31.cloned.1.call-update) | async-done | bytes 995344 | tf_op jit(solution)/shard_map/reduce_scatter | solution.py:450
  341.9 62.6 %reduce-scatter.39.cloned.1.call-done = bf16[288,2304]{1,0:T(8,128)(2,1)} async-done(((bf16[1152,2304]{1,0:T(8,128)(2,1)}), bf16[288,2304]{1,0:T(8,128)(2,1)}) %reduce-scatter.39.cloned.1.call-update) | async-done | bytes 1327120 | tf_op jit(solution)/shard_map/reduce_scatter | solution.py:450
  407.4 67.4 %reduce-scatter.41.cloned.1.call-done = bf16[1152,576]{1,0:T(8,128)(2,1)} async-done(((bf16[4608,576]{1,0:T(8,128)(2,1)}), bf16[1152,576]{1,0:T(8,128)(2,1)}) %reduce-scatter.41.cloned.1.call-update) | async-done | bytes 1327120 | tf_op jit(solution)/shard_map/reduce_scatter | solution.py:450
  480.0 6.1 fusion.33
  488.1 28.6 %all-reduce.2 = f32[6912]{0:T(1024)S(1)} all-reduce(f32[6912]{0:T(1024)S(1)} %reshape.130), channel_id=2, replica_groups=mesh['dp'=4,'sp'=8] {'sp'}, use_global_device_ids=true, to_apply=%region_16.17.clone | all-reduce | flops 6912 | bytes 55296
  516.8 8.8 %all-reduce.3 = f32[864]{0:T(1024)S(1)} all-reduce(f32[864]{0:T(1024)S(1)} %dynamic-slice.2), channel_id=3, replica_groups=mesh['dp'=4,'sp'=8] {'dp'}, use_global_device_ids=true, to_apply=%region_17.18.clone | all-reduce | flops 864 | bytes 6912
  530.6 19.8 %reduce-scatter.47.cloned.1.call-done = bf16[144,288]{1,0:T(8,128)(2,1)} async-done(((bf16[576,288]{1,0:T(8,128)(2,1)}), bf16[144,288]{1,0:T(8,128)(2,1)}) %reduce-scatter.47.cloned.1.call-update) | async-done | bytes 82960
  552.1 20.0 %reduce-scatter.53.cloned.1.call-done = bf16[144,288]{1,0:T(8,128)(2,1)} async-done(((bf16[576,288]{1,0:T(8,128)(2,1)}), bf16[144,288]{1,0:T(8,128)(2,1)}) %reduce-scatter.53.cloned.1.call-update) | async-done | bytes 82960
  573.9 30.3 %reduce-scatter.43.cloned.1.call-done = bf16[432,288]{1,0:T(8,128)(2,1)} async-done(((bf16[1728,288]{1,0:T(8,128)(2,1)}), bf16[432,288]{1,0:T(8,128)(2,1)}) %reduce-scatter.43.cloned.1.call-update) | async-done | bytes 248848
  606.2 37.6 %reduce-scatter.55.cloned.1.call-done = bf16[576,288]{1,0:T(8,128)(2,1)} async-done(((bf16[2304,288]{1,0:T(8,128)(2,1)}), bf16[576,288]{1,0:T(8,128)(2,1)}) %reduce-scatter.55.cloned.1.call-update) | async-done | bytes 331792
  646.1 30.8 %reduce-scatter.57.cloned.1.call-done = bf16[144,1152]{1,0:T(8,128)(2,1)} async-done(((bf16[576,1152]{1,0:T(8,128)(2,1)}), bf16[144,1152]{1,0:T(8,128)(2,1)}) %reduce-scatter.57.cloned.1.call-update) | async-done | bytes 331792
  (318 shorter events, 137.0 us)
Async XLA Ops:
  7.2 279.8 %reduce-scatter.49.cloned.1.call-start = ((), (), s32[]{:S(2)}) async-start(), calls=%async_computation.23 | async-start | bytes 1327104
  19.5 12.6 %collective-permute-start = (bf16[256,1152]{1,0:T(8,128)(2,1)S(1)}, bf16[256,1152]{1,0:T(8,128)(2,1)S(1)}, u32[]{:S(2)}, u32[]{:S(2)}) collective-permute-start(bf16[256,1152]{1,0:T(8,128)(2,1)S(1)} %fusion.27.x0_ref), channel_id=1, source_target_pairs={{1,0},{2,1},{3,2},{4,3},{5,4},{6,5},{7,6},{9,8},{10,9},{11,10},{12... | collective-permute-start | bytes 1769480 | tf_op jit(solution)/shard_map/ppermute | solution.py:423
  21.1 13.3 %collective-permute-start.1 = (bf16[256,1152]{1,0:T(8,128)(2,1)S(1)}, bf16[256,1152]{1,0:T(8,128)(2,1)}, u32[]{:S(2)}, u32[]{:S(2)}) collective-permute-start(bf16[256,1152]{1,0:T(8,128)(2,1)S(1)} %fusion.27.x0_ref), channel_id=1, source_target_pairs={{0,1},{1,2},{2,3},{3,4},{4,5},{5,6},{6,7},{8,9},{9,10},{10,11},{11... | collective-permute-start | bytes 1769480 | tf_op jit(solution)/shard_map/ppermute | solution.py:422
  32.2 8.4 %collective-permute-start.4 = (bf16[256,1152]{1,0:T(8,128)(2,1)S(1)}, bf16[256,1152]{1,0:T(8,128)(2,1)}, u32[]{:S(2)}, u32[]{:S(2)}) collective-permute-start(bf16[256,1152]{1,0:T(8,128)(2,1)S(1)} %collective-permute-done), channel_id=1, source_target_pairs={{1,0},{2,1},{3,2},{4,3},{5,4},{6,5},{7,6},{9,8},{10,9},{11,10},{12... | collective-permute-start | bytes 1769480 | tf_op jit(solution)/shard_map/ppermute | solution.py:423
  34.4 12.7 %collective-permute-start.2 = (bf16[256,1152]{1,0:T(8,128)(2,1)}, bf16[256,1152]{1,0:T(8,128)(2,1)}, u32[]{:S(2)}, u32[]{:S(2)}) collective-permute-start(bf16[256,1152]{1,0:T(8,128)(2,1)} %collective-permute-done.1), channel_id=1, source_target_pairs={{0,1},{1,2},{2,3},{3,4},{4,5},{5,6},{6,7},{8,9},{9,10},{10,11},{11... | collective-permute-start | bytes 1769480 | tf_op jit(solution)/shard_map/ppermute | solution.py:422
  40.6 15.0 %collective-permute-start.5 = (bf16[256,1152]{1,0:T(8,128)(2,1)}, bf16[256,1152]{1,0:T(8,128)(2,1)}, u32[]{:S(2)}, u32[]{:S(2)}) collective-permute-start(bf16[256,1152]{1,0:T(8,128)(2,1)} %collective-permute-done.4), channel_id=1, source_target_pairs={{1,0},{2,1},{3,2},{4,3},{5,4},{6,5},{7,6},{9,8},{10,9},{11,10},{12... | collective-permute-start | bytes 1769480 | tf_op jit(solution)/shard_map/ppermute | solution.py:423
  47.2 9.6 %collective-permute-start.3 = (bf16[256,1152]{1,0:T(8,128)(2,1)}, bf16[256,1152]{1,0:T(8,128)(2,1)S(1)}, u32[]{:S(2)}, u32[]{:S(2)}) collective-permute-start(bf16[256,1152]{1,0:T(8,128)(2,1)} %collective-permute-done.2), channel_id=1, source_target_pairs={{0,1},{1,2},{2,3},{3,4},{4,5},{5,6},{6,7},{8,9},{9,10},{10,11},{11... | collective-permute-start | bytes 1769480 | tf_op jit(solution)/shard_map/ppermute | solution.py:422
  139.7 150.0 %reduce-scatter.33.cloned.1.call-start = ((), (), s32[]{:S(2)}) async-start(), calls=%async_computation.15 | async-start | bytes 1843200 | tf_op jit(solution)/shard_map/reduce_scatter | solution.py:450
  139.7 12.7 %collective-permute-start.14 = (bf16[256,1152]{1,0:T(8,128)(2,1)S(1)}, bf16[256,1152]{1,0:T(8,128)(2,1)S(1)}, u32[]{:S(2)}, u32[]{:S(2)}) collective-permute-start(bf16[256,1152]{1,0:T(8,128)(2,1)S(1)} %get-tuple-element.17.x0_ref), channel_id=1, source_target_pairs={{0,1},{1,0},{2,3},{3,2},{4,5},{5,4},{6,7},{7,6},{8,9},{9,8},{10,11... | collective-permute-start | bytes 1769480 | tf_op jit(solution)/shard_map/ppermute | solution.py:445
  155.5 136.2 %reduce-scatter.35.cloned.1.call-start = ((), (), s32[]{:S(2)}) async-start(), calls=%async_computation.16 | async-start | bytes 1843200 | tf_op jit(solution)/shard_map/reduce_scatter | solution.py:450
  163.6 130.2 %reduce-scatter.37.cloned.1.call-start = ((), (), s32[]{:S(2)}) async-start(), calls=%async_computation.17 | async-start | bytes 1843200 | tf_op jit(solution)/shard_map/reduce_scatter | solution.py:450
  165.7 5.4 collective-permute-start.6
  167.3 21.4 %collective-permute-start.7 = (bf16[272,1152]{1,0:T(8,128)(2,1)S(1)}, bf16[272,1152]{1,0:T(8,128)(2,1)}, u32[]{:S(2)}, u32[]{:S(2)}) collective-permute-start(bf16[272,1152]{1,0:T(8,128)(2,1)S(1)} %pad_maximum_fusion.2.pack0_ref), channel_id=1, source_target_pairs={{0,1},{1,2},{2,3},{3,4},{4,5},{5,6},{6,7},{8,9},{9,10},{10,11},{11... | collective-permute-start | bytes 1880072 | tf_op jit(solution)/shard_map/ppermute | solution.py:422
  171.2 20.7 %collective-permute-start.10 = (bf16[272,1152]{1,0:T(8,128)(2,1)S(1)}, bf16[272,1152]{1,0:T(8,128)(2,1)}, u32[]{:S(2)}, u32[]{:S(2)}) collective-permute-start(bf16[272,1152]{1,0:T(8,128)(2,1)S(1)} %collective-permute-done.6), channel_id=1, source_target_pairs={{1,0},{2,1},{3,2},{4,3},{5,4},{6,5},{7,6},{9,8},{10,9},{11,10},{12... | collective-permute-start | bytes 1880072 | tf_op jit(solution)/shard_map/ppermute | solution.py:423
  172.4 27.8 %collective-permute-start.18 = (bf16[256,1152]{1,0:T(8,128)(2,1)}, bf16[256,1152]{1,0:T(8,128)(2,1)S(1)}, u32[]{:S(2)}, u32[]{:S(2)}) collective-permute-start(bf16[256,1152]{1,0:T(8,128)(2,1)} %shard_map.214.x0_ref), channel_id=1, source_target_pairs={{0,1},{1,0},{2,3},{3,2},{4,5},{5,4},{6,7},{7,6},{8,9},{9,8},{10,11... | collective-permute-start | bytes 1769480 | tf_op jit(solution)/shard_map/ppermute | solution.py:445
  188.6 11.7 %collective-permute-start.19 = (bf16[256,576]{1,0:T(8,128)(2,1)S(1)}, bf16[256,576]{1,0:T(8,128)(2,1)S(1)}, u32[]{:S(2)}, u32[]{:S(2)}) collective-permute-start(bf16[256,576]{1,0:T(8,128)(2,1)S(1)} %get-tuple-element.100), channel_id=1, source_target_pairs={{0,1},{1,0},{2,3},{3,2},{4,5},{5,4},{6,7},{7,6},{8,9},{9,8},{10,11... | collective-permute-start | bytes 884744 | tf_op jit(solution)/shard_map/ppermute | solution.py:445
  188.7 16.1 %collective-permute-start.8 = (bf16[272,1152]{1,0:T(8,128)(2,1)}, bf16[272,1152]{1,0:T(8,128)(2,1)}, u32[]{:S(2)}, u32[]{:S(2)}) collective-permute-start(bf16[272,1152]{1,0:T(8,128)(2,1)} %collective-permute-done.7), channel_id=1, source_target_pairs={{0,1},{1,2},{2,3},{3,4},{4,5},{5,6},{6,7},{8,9},{9,10},{10,11},{11... | collective-permute-start | bytes 1880072 | tf_op jit(solution)/shard_map/ppermute | solution.py:422
  191.9 22.6 %collective-permute-start.11 = (bf16[272,1152]{1,0:T(8,128)(2,1)}, bf16[272,1152]{1,0:T(8,128)(2,1)}, u32[]{:S(2)}, u32[]{:S(2)}) collective-permute-start(bf16[272,1152]{1,0:T(8,128)(2,1)} %collective-permute-done.10), channel_id=1, source_target_pairs={{1,0},{2,1},{3,2},{4,3},{5,4},{6,5},{7,6},{9,8},{10,9},{11,10},{12... | collective-permute-start | bytes 1880072 | tf_op jit(solution)/shard_map/ppermute | solution.py:423
  204.7 134.7 %reduce-scatter.31.cloned.1.call-start = ((), (), s32[]{:S(2)}) async-start(), calls=%async_computation.14 | async-start | bytes 5160960 | tf_op jit(solution)/shard_map/reduce_scatter | solution.py:450
  204.8 10.9 %collective-permute-start.9 = (bf16[272,1152]{1,0:T(8,128)(2,1)}, bf16[272,1152]{1,0:T(8,128)(2,1)S(1)}, u32[]{:S(2)}, u32[]{:S(2)}) collective-permute-start(bf16[272,1152]{1,0:T(8,128)(2,1)} %collective-permute-done.8), channel_id=1, source_target_pairs={{0,1},{1,2},{2,3},{3,4},{4,5},{5,6},{6,7},{8,9},{9,10},{10,11},{11... | collective-permute-start | bytes 1880072 | tf_op jit(solution)/shard_map/ppermute | solution.py:422
  230.3 15.8 %collective-permute-start.13 = (bf16[256,1728]{0,1:T(8,128)(2,1)}, bf16[256,1728]{0,1:T(8,128)(2,1)}, u32[]{:S(2)}, u32[]{:S(2)}) collective-permute-start(bf16[256,1728]{0,1:T(8,128)(2,1)} %copy.53), channel_id=1, source_target_pairs={{0,1},{1,0},{2,3},{3,2},{4,5},{5,4},{6,7},{7,6},{8,9},{9,8},{10,11... | collective-permute-start | bytes 2654216 | tf_op jit(solution)/shard_map/ppermute | solution.py:445
  242.9 4.7 collective-permute-start.12
  253.2 151.3 %reduce-scatter.39.cloned.1.call-start = ((), (), s32[]{:S(2)}) async-start(), calls=%async_computation.18 | async-start | bytes 6635520 | tf_op jit(solution)/shard_map/reduce_scatter | solution.py:450
  273.1 201.6 %reduce-scatter.41.cloned.1.call-start = ((), (), s32[]{:S(2)}) async-start(), calls=%async_computation.19 | async-start | bytes 7372800 | tf_op jit(solution)/shard_map/reduce_scatter | solution.py:450
  274.8 5.0 collective-permute-start.22
  286.9 239.3 %reduce-scatter.51.cloned.1.call-start = ((), (), s32[]{:S(2)}) async-start(), calls=%async_computation.24 | async-start | bytes 1105920
  289.7 239.1 %reduce-scatter.45.cloned.1.call-start = ((), (), s32[]{:S(2)}) async-start(), calls=%async_computation.21 | async-start | bytes 552960
  291.7 258.6 %reduce-scatter.47.cloned.1.call-start = ((), (), s32[]{:S(2)}) async-start(), calls=%async_computation.22 | async-start | bytes 552960
  293.7 278.4 %reduce-scatter.53.cloned.1.call-start = ((), (), s32[]{:S(2)}) async-start(), calls=%async_computation.25 | async-start | bytes 552960
  295.9 308.4 %reduce-scatter.43.cloned.1.call-start = ((), (), s32[]{:S(2)}) async-start(), calls=%async_computation.20 | async-start | bytes 1658880
  341.9 301.9 %reduce-scatter.55.cloned.1.call-start = ((), (), s32[]{:S(2)}) async-start(), calls=%async_computation.26 | async-start | bytes 2211840
  407.3 269.5 %reduce-scatter.57.cloned.1.call-start = ((), (), s32[]{:S(2)}) async-start(), calls=%async_computation.27 | async-start | bytes 1658880
  (74 other events, 1087.5 us)
Sparse Core Ops, SparseCore 0:
  139.8 45.7 reduce-scatter.48
  188.6 28.5 reduce-scatter.32
  220.4 30.3 reduce-scatter.34
  253.6 30.3 reduce-scatter.36
  287.2 52.1 reduce-scatter.30
  342.5 61.9 reduce-scatter.38
  407.8 66.9 reduce-scatter.40
  478.0 26.6 reduce-scatter.50
  507.7 21.0 reduce-scatter.44
  530.9 19.3 reduce-scatter.46
  552.7 19.3 reduce-scatter.52
  574.3 29.9 reduce-scatter.42
  606.6 37.1 reduce-scatter.54
  646.1 30.7 reduce-scatter.56
